TPU v7x, 512 devices: a whole 4x8x8 slice. The times are simulated.
512 devices in a mesh: head: 8 (over x, core), ctx: 64 (over y, z).
Axes of the slice: x: 4, y: 8, z: 8, core: 2. Of those that a mesh axis runs over, the one named last changes fastest.
Arguments:
- queries: bfloat16 [512, 1024], P(None, 'head'), may hold values from -32 to 32
- keys: bfloat16 [512, 65536], P('head', 'ctx'), may hold values from -6 to 6
- values: bfloat16 [512, 65536], P('head', 'ctx'), may hold values from -6 to 6
- positions: float32 [3, 65536], P(None, 'ctx'), may hold values from 0 to 4
- falloff: float32 [8], P('head'), may hold values from 0.05 to 1
- query_ids: int32 [1024], replicated, may hold values from 0 to 65535
- cotangent: bfloat16 [512, 1024], P(None, 'head'), may hold values from -6 to 6
Outputs:
- attended: bfloat16 [512, 1024], P('head')
- query_grad: float32 [512, 1024], P('head')
- forces: float32 [3, 1024], replicated
All inputs are finite; a program needn't handle non-finite values.
Results may differ from a plain program's by a relative error of at most 0.013.
Values may be sent and summed in bfloat16 or wider, within the bound.
A program may use at most 128 MiB of HBM per device.

v0:
```python
import math
import jax
import jax.numpy as jnp
from jax import lax
from jax.sharding import PartitionSpec as P

HEAD_DIM = 64


def shards(queries, keys, values, positions, falloff, query_ids, cotangent):
    scaling = HEAD_DIM ** (-0.5)
    query_rows, grad_rows = (
        lax.all_to_all(queries, "head", split_axis=0, concat_axis=1, tiled=True),
        lax.all_to_all(cotangent, "head", split_axis=0, concat_axis=1, tiled=True),
    )
    query_count = query_rows.shape[1]
    head_count = query_rows.shape[0] // HEAD_DIM
    key_count = keys.shape[1]
    key_block = math.gcd(key_count, 512)
    block_count = key_count // key_block
    query_heads = query_rows.reshape(head_count, HEAD_DIM, query_count)
    local_index = query_ids - lax.axis_index("ctx") * key_count
    owner_mask = jnp.logical_and(local_index >= 0, local_index < key_count)
    picked = jnp.take(positions, jnp.clip(local_index, 0, key_count - 1), axis=1)
    picked = picked * owner_mask.astype(jnp.float32)[None, :]
    query_place = lax.psum(picked, "ctx")

    def block_parts(index):
        offset = index * key_block
        key_heads = lax.dynamic_slice_in_dim(keys, offset, key_block, 1).reshape(
            head_count, HEAD_DIM, key_block
        )
        value_heads = lax.dynamic_slice_in_dim(values, offset, key_block, 1).reshape(
            head_count, HEAD_DIM, key_block
        )
        place_part = lax.dynamic_slice_in_dim(positions, offset, key_block, 1)
        dots = (
            jnp.einsum("hcq,hck->hqk", query_heads, key_heads, preferred_element_type=jnp.float32)
            * scaling
        )
        dist = jnp.zeros((query_count, key_block), jnp.float32)
        for axis_id in range(3):
            gap = query_place[axis_id][:, None] - place_part[axis_id][None, :]
            dist = dist + gap * gap
        scores = dots - falloff[:, None, None] * dist[None]
        return (scores, key_heads, value_heads, place_part)

    def forward_step(carry, index):
        run_max, run_total, accum = carry
        scores, key_heads, value_heads, place_part = block_parts(index)
        new_max = jnp.maximum(run_max, jnp.max(scores, axis=-1))
        shrink = jnp.exp(run_max - new_max)
        weights = jnp.exp(scores - new_max[..., None])
        accum = accum * shrink[:, None, :] + jnp.einsum(
            "hck,hqk->hcq",
            value_heads,
            weights.astype(jnp.bfloat16),
            preferred_element_type=jnp.float32,
        )
        run_total = run_total * shrink + jnp.sum(weights, axis=-1)
        return ((new_max, run_total, accum), None)

    start = (
        jnp.full((head_count, query_count), -jnp.inf, jnp.float32),
        jnp.zeros((head_count, query_count), jnp.float32),
        jnp.zeros((head_count, HEAD_DIM, query_count), jnp.float32),
    )
    (row_max, row_total, accum), _ = lax.scan(
        forward_step, start, jnp.arange(block_count, dtype=jnp.int32)
    )
    global_max = lax.pmax(row_max, "ctx")
    factor = jnp.exp(row_max - global_max)
    row_total, accum = lax.psum((row_total * factor, accum * factor[:, None, :]), "ctx")
    row_max = global_max
    grad_heads = grad_rows.reshape(head_count, HEAD_DIM, query_count)
    output32 = accum / row_total[:, None, :]
    attended = output32.reshape(head_count * HEAD_DIM, query_count).astype(jnp.bfloat16)
    log_total = row_max + jnp.log(row_total)
    row_delta = jnp.sum(grad_heads.astype(jnp.float32) * output32, axis=1)

    def backward_step(carry, index):
        grad_part, force_part = carry
        scores, key_heads, value_heads, place_part = block_parts(index)
        probs = jnp.exp(scores - log_total[..., None])
        grad_probs = jnp.einsum(
            "hcq,hck->hqk", grad_heads, value_heads, preferred_element_type=jnp.float32
        )
        grad_scores = probs * (grad_probs - row_delta[..., None])
        grad_part = (
            grad_part
            + jnp.einsum(
                "hck,hqk->hcq",
                key_heads,
                grad_scores.astype(jnp.bfloat16),
                preferred_element_type=jnp.float32,
            )
            * scaling
        )
        pull = jnp.sum(2.0 * falloff[:, None, None] * grad_scores, axis=0)
        toward = lax.dot_general(
            place_part, pull, (((1,), (1,)), ((), ())), precision=lax.Precision.HIGHEST
        )
        force_part = force_part - query_place * jnp.sum(pull, axis=-1)[None, :] + toward
        return ((grad_part, force_part), None)

    start = (
        jnp.zeros((head_count, HEAD_DIM, query_count), jnp.float32),
        jnp.zeros((3, query_count), jnp.float32),
    )
    (grad_part, force_part), _ = lax.scan(
        backward_step, start, jnp.arange(block_count, dtype=jnp.int32)
    )
    query_grad, head_force = lax.psum((grad_part, force_part), "ctx")
    forces = lax.psum(head_force, "head")
    return (attended, query_grad.reshape(head_count * HEAD_DIM, query_count), forces)


def solution(mesh):
    return jax.shard_map(
        shards,
        mesh=mesh,
        in_specs=(
            P(None, "head"),
            P("head", "ctx"),
            P("head", "ctx"),
            P(None, "ctx"),
            P("head"),
            P(),
            P(None, "head"),
        ),
        out_specs=(P("head", None), P("head", None), P()),
        check_vma=False,
    )
```

profile of v0, /device:TPU:32, one launch (start us, length us, event | category | flops | bytes accessed | tf_op | source)
XLA Modules:
  0.0 926.0 jit_solution(12605305617123553743)
XLA Ops:
  7.2 4.3 all-to-all-start
  11.5 0.0 copy-start.1
  11.5 0.0 copy-start.2
  11.5 0.0 copy-start.3
  11.5 0.8 compare_and_fusion
  12.3 0.7 fusion.35
  13.0 0.9 copy.19
  13.9 2.8 gather_fusion
  16.7 0.3 multiply_bitcast_fusion
  17.1 285.8 %psum.42 = f32[3,1024]{0,1:T(8,128)S(1)} all-reduce(f32[3,1024]{0,1:T(8,128)S(1)} %multiply_bitcast_fusion), channel_id=1, replica_groups=mesh['head'=8,'ctx'=64] {'ctx'}, use_global_device_ids=true, to_apply=%region_0.1 | all-reduce | flops 3072 | bytes 24576 | tf_op jit(solution)/shard_map/psum | solution.py:26
  302.8 0.2 copy.20
  303.0 0.0 all-to-all-done
  303.0 4.8 all-to-all-start.1
  307.8 0.0 all-reduce.3.cloned.1.call-start
  307.9 0.1 copy.18
  308.0 0.1 reshape.142
  308.1 0.0 copy-done.1
  308.1 0.0 copy-done.2
  308.1 0.0 copy-done.3
  308.1 7.8 while.29
  308.1 0.6 dynamic_slice.63
  309.4 0.1 constant_dynamic-slice_fusion.4
  309.5 1.6 fusion.61
  311.1 0.3 fusion.63
  311.5 0.5 fusion.65
  312.0 0.6 dynamic_slice.63
  313.2 0.1 constant_dynamic-slice_fusion.4
  313.3 1.6 fusion.61
  315.0 0.3 fusion.63
  315.4 0.5 fusion.65
  315.9 138.0 %pmax.7 = f32[1,1024]{1,0:T(1,128)S(1)} all-reduce(f32[1,1024]{1,0:T(1,128)S(1)} %get-tuple-element.188), channel_id=1, replica_groups=mesh['head'=8,'ctx'=64] {'ctx'}, use_global_device_ids=true, to_apply=%region_5.6 | all-reduce | flops 1024 | bytes 8192 | tf_op jit(solution)/shard_map/pmax | solution.py:71
  453.9 0.7 broadcast_multiply_fusion
  454.6 0.0 all-reduce.3.cloned.1.call-update
  454.6 0.0 all-reduce.5.cloned.1.call-start
  455.4 0.0 all-to-all-done.1
  455.4 0.1 copy.21
  455.5 0.1 reshape.143
  455.5 140.0 %psum.44 = f32[1,1024]{1,0:T(1,128)S(1)} all-reduce(f32[1,1024]{1,0:T(1,128)S(1)} %get-tuple-element.400), channel_id=1, replica_groups=mesh['head'=8,'ctx'=64] {'ctx'}, use_global_device_ids=true, to_apply=%region_7.8 | all-reduce | flops 1024 | bytes 8192 | tf_op jit(solution)/shard_map/psum | solution.py:73
  595.6 7.2 all-reduce.3.cloned.1.call-done
  602.8 1.7 multiply_reduce_fusion.1
  604.4 10.9 %while.30 = (s32[]{:T(128)}, f32[1,64,1024]{2,1,0:T(8,128)S(1)}, f32[3,1024]{1,0:T(4,128)S(1)}, s32[2]{0:T(128)S(1)}, bf16[64,1024]{1,0:T(8,128)(2,1)S(1)}, /*in...) while((s32[]{:T(128)}, f32[1,64,1024]{2,1,0:T(8,128)S(1)}, ...), condition=%wide.region_11.12_spmd.clone, body=%wide.region_9.11_spmd.clone.sunk | while | flops 229846016 | bytes 11594042 | solution.py:110
  604.4 0.6 dynamic_slice.68
  605.7 0.1 constant_dynamic-slice_fusion.5
  605.8 0.5 fusion.73
  606.3 2.1 multiply_reduce_fusion.3
  608.4 1.2 fusion.75
  609.6 0.3 fusion.74
  609.9 0.6 dynamic_slice.68
  611.1 0.1 constant_dynamic-slice_fusion.5
  611.2 0.5 fusion.73
  611.7 2.1 multiply_reduce_fusion.3
  613.9 1.2 fusion.75
  615.0 0.3 fusion.74
  615.4 0.0 copy-start
  615.4 0.7 copy-done
  616.1 0.0 all-reduce.5.cloned.1.call-update
  616.1 277.3 %psum.46 = f32[3,1024]{1,0:T(4,128)S(1)} all-reduce(f32[3,1024]{1,0:T(4,128)S(1)} %get-tuple-element.191), channel_id=1, replica_groups=mesh['head'=8,'ctx'=64] {'ctx'}, use_global_device_ids=true, to_apply=%region_13.14 | all-reduce | flops 3072 | bytes 24576 | tf_op jit(solution)/shard_map/psum | solution.py:113
  893.4 24.1 %psum.47 = f32[3,1024]{1,0:T(4,128)} all-reduce(f32[3,1024]{1,0:T(4,128)S(1)} %psum.46), channel_id=1, replica_groups=mesh['head'=8,'ctx'=64] {'head'}, use_global_device_ids=true, to_apply=%region_14.15 | all-reduce | flops 3072 | bytes 24576 | tf_op jit(solution)/shard_map/psum | solution.py:114
  917.5 0.0 all-reduce.5.cloned.1.call-done
  917.5 1.7 copy.47
  (19 shorter events, 0.2 us)
Async XLA Ops:
  7.2 295.9 %all-to-all-start = ((bf16[8,64,128]{2,1,0:T(8,128)(2,1)}), bf16[8,64,128]{2,1,0:T(8,128)(2,1)S(1)}, u32[]{:S(2)}, u32[]{:S(2)}) async-start(bf16[8,64,128]{2,1,0:T(8,128)(2,1)} %bitcast.132), calls=%async_computation | async-start | bytes 262144 | tf_op jit(solution)/shard_map/all_to_all | solution.py:13
  11.5 296.6 %copy-start.1 = (bf16[64,1024]{1,0:T(8,128)(2,1)S(1)}, bf16[64,1024]{1,0:T(8,128)(2,1)}, u32[]{:S(2)}) copy-start(bf16[64,1024]{1,0:T(8,128)(2,1)} %param.12) | copy-start | bytes 393220
  11.5 296.6 %copy-start.2 = (f32[3,1024]{1,0:T(4,128)S(1)}, f32[3,1024]{1,0:T(4,128)}, u32[]{:S(2)}) copy-start(f32[3,1024]{1,0:T(4,128)} %param.14) | copy-start | bytes 36868
  11.5 296.6 %copy-start.3 = (bf16[64,1024]{1,0:T(8,128)(2,1)S(1)}, bf16[64,1024]{1,0:T(8,128)(2,1)}, u32[]{:S(2)}) copy-start(bf16[64,1024]{1,0:T(8,128)(2,1)} %param.13) | copy-start | bytes 393220
  303.0 152.3 %all-to-all-start.1 = ((bf16[8,64,128]{2,1,0:T(8,128)(2,1)}), bf16[8,64,128]{2,1,0:T(8,128)(2,1)S(1)}, u32[]{:S(2)}, u32[]{:S(2)}) async-start(bf16[8,64,128]{2,1,0:T(8,128)(2,1)} %bitcast.6), calls=%async_computation.1 | async-start | bytes 262144 | tf_op jit(solution)/shard_map/all_to_all | solution.py:14
  307.8 294.9 %all-reduce.3.cloned.1.call-start = ((), (), s32[]{:S(2)}) async-start(), calls=%async_computation.2 | async-start | bytes 524288 | tf_op jit(solution)/shard_map/psum | solution.py:73
  454.6 462.9 %all-reduce.5.cloned.1.call-start = ((), (), s32[]{:S(2)}) async-start(), calls=%async_computation.3 | async-start | bytes 524288 | tf_op jit(solution)/shard_map/psum | solution.py:113
  615.4 0.7 copy-start
Sparse Core Ops, SparseCore 0:
  454.8 147.9 all-reduce.2
  616.2 148.4 all-reduce.4
where the time goes:
time: 927 us; the launch traced here: 926 us
  blocking collectives  865 us (93%)
  between operations  14.9 us (2%)
  matrix products  12.4 us (1%)
  local copies, waits for them, and re-layouts  9.35 us (1%)
    psum x1, blocking collectives, shards(): query_place = lax.psum(picked, 'ctx')  286 us
    psum x1, blocking collectives, shards(): query_grad, head_force = lax.psum((grad_part, force_part), 'ctx')  277 us
    psum x1, blocking collectives, shards(): lax.psum((row_total * factor, accum * factor[:, None, :]), 'ctx')  140 us
    pmax x1, blocking collectives, shards(): global_max = lax.pmax(row_max, 'ctx')  138 us
    psum x1, blocking collectives, shards(): forces = lax.psum(head_force, 'head')  24.1 us
  transfers between devices with their start and end apart: 4, of which 1 were waited for; matrix products, arithmetic and copies ran while one was open for 1% of the time, Pallas kernels for 0%

commit v1 on v0

--- a/solution.py
+++ b/solution.py
@@ -23,7 +23,7 @@
     owner_mask = jnp.logical_and(local_index >= 0, local_index < key_count)
     picked = jnp.take(positions, jnp.clip(local_index, 0, key_count - 1), axis=1)
     picked = picked * owner_mask.astype(jnp.float32)[None, :]
-    query_place = lax.psum(picked, "ctx")
+    query_place = jnp.sum(lax.all_gather(picked, "ctx"), axis=0)
 
     def block_parts(index):
         offset = index * key_block

time: 927 us -> 698 us (0.75)
  blocking collectives: 865 us -> 636 us
    psum x1 -> x0, blocking collectives: 286 us -> none  [shards(): query_place = lax.psum(picked, 'ctx')]
    all_gather x0 -> x1, blocking collectives: none -> 55.7 us  [shards(): query_place = jnp.sum(lax.all_gather(picked, 'ctx'), axis=0)]
  transfers between devices with their start and end apart: 4 -> 4, of which waited for: 1 -> 1; matrix products, arithmetic and copies ran while one was open for 1% -> 2% of each run, Pallas kernels for 0% -> 0%
where the time goes in v1:
time: 698 us; the launch traced here: 697 us
  blocking collectives  636 us (91%)
  between operations  14.9 us (2%)
  matrix products  12.4 us (2%)
  local copies, waits for them, and re-layouts  9.42 us (1%)
  starting transfers between devices  9.39 us (1%)
  waiting for transfers between devices  7.91 us (1%)
    psum x1, blocking collectives, shards(): query_grad, head_force = lax.psum((grad_part, force_part), 'ctx')  277 us
    pmax x1, blocking collectives, shards(): global_max = lax.pmax(row_max, 'ctx')  141 us
    psum x1, blocking collectives, shards(): lax.psum((row_total * factor, accum * factor[:, None, :]), 'ctx')  138 us
    all_gather x1, blocking collectives, shards(): query_place = jnp.sum(lax.all_gather(picked, 'ctx'), axis=0)  55.7 us
    psum x1, blocking collectives, shards(): forces = lax.psum(head_force, 'head')  24.1 us
  transfers between devices with their start and end apart: 4, of which 1 were waited for; matrix products, arithmetic and copies ran while one was open for 2% of the time, Pallas kernels for 0%

profile of v1, /device:TPU:32, one launch (start us, length us, event | category | flops | bytes accessed | tf_op | source)
XLA Modules:
  0.0 697.4 jit_solution(12087987087016708597)
XLA Ops:
  7.2 4.3 all-to-all-start
  11.5 0.7 and_convert_fusion
  12.2 0.7 fusion.36
  12.9 0.0 copy-start.1
  12.9 0.0 copy-start.2
  12.9 0.0 copy-start.3
  12.9 1.0 copy.26
  13.9 2.8 gather_fusion
  16.7 0.2 copy.27
  17.0 55.7 %all_gather.4 = f32[64,3,1024]{2,1,0:T(4,128)S(1)} all-gather(f32[1,3,1024]{2,1,0:T(4,128)S(1)} %copy.28), channel_id=1, replica_groups=mesh['head'=8,'ctx'=64] {'ctx'}, dimensions={0}, use_global_device_ids=true | all-gather | bytes 798720 | tf_op jit(solution)/shard_map/all_gather | solution.py:26
  72.7 0.2 reduce_sum.45
  72.9 0.0 all-to-all-done
  72.9 5.0 all-to-all-start.1
  77.9 0.0 all-reduce.3.cloned.1.call-start
  77.9 0.1 copy.25
  78.0 0.1 reshape.194
  78.1 0.0 copy-done.1
  78.1 0.0 copy-done.2
  78.1 0.0 copy-done.3
  78.1 7.8 %while.29 = (s32[]{:T(128)}, f32[1,1024]{1,0:T(1,128)S(1)}, f32[1,1024]{1,0:T(1,128)S(1)}, f32[1,64,1024]{2,1,0:T(8,128)S(1)}, s32[2]{0:T(128)S(1)}, /*index=5*/...) while((s32[]{:T(128)}, f32[1,1024]{1,0:T(1,128)S(1)}, ...), condition=%wide.region_4.5_spmd.clone, body=%wide.region_1.4_spmd.clone.sunk | while | flops 142808064 | bytes 7198995 | solution.py:68
  78.1 0.6 dynamic_slice.63
  79.4 0.1 constant_dynamic-slice_fusion.4
  79.5 1.6 fusion.62
  81.2 0.3 fusion.64
  81.5 0.5 fusion.66
  82.0 0.6 dynamic_slice.63
  83.3 0.1 constant_dynamic-slice_fusion.4
  83.4 1.6 fusion.62
  85.0 0.3 fusion.64
  85.4 0.5 fusion.66
  85.9 140.6 %pmax.7 = f32[1,1024]{1,0:T(1,128)S(1)} all-reduce(f32[1,1024]{1,0:T(1,128)S(1)} %get-tuple-element.188), channel_id=1, replica_groups=mesh['head'=8,'ctx'=64] {'ctx'}, use_global_device_ids=true, to_apply=%region_5.6 | all-reduce | flops 1024 | bytes 8192 | tf_op jit(solution)/shard_map/pmax | solution.py:71
  226.6 0.7 broadcast_multiply_fusion
  227.3 0.0 all-reduce.3.cloned.1.call-update
  227.3 0.0 all-reduce.5.cloned.1.call-start
  228.0 0.0 all-to-all-done.1
  228.1 0.1 copy.31
  228.2 0.1 reshape.195
  228.2 138.0 %psum.36 = f32[1,1024]{1,0:T(1,128)S(1)} all-reduce(f32[1,1024]{1,0:T(1,128)S(1)} %get-tuple-element.400), channel_id=1, replica_groups=mesh['head'=8,'ctx'=64] {'ctx'}, use_global_device_ids=true, to_apply=%region_7.8 | all-reduce | flops 1024 | bytes 8192 | tf_op jit(solution)/shard_map/psum | solution.py:73
  366.3 7.9 %all-reduce.3.cloned.1.call-done = f32[1,64,1024]{2,1,0:T(8,128)} async-done(((f32[1,64,1024]{2,1,0:T(8,128)}), f32[1,64,1024]{2,1,0:T(8,128)}) %all-reduce.3.cloned.1.call-update) | async-done | bytes 262160 | tf_op jit(solution)/shard_map/psum | solution.py:73
  374.1 1.7 multiply_reduce_fusion.1
  375.8 10.9 %while.30 = (s32[]{:T(128)}, f32[1,64,1024]{2,1,0:T(8,128)S(1)}, f32[3,1024]{1,0:T(4,128)S(1)}, s32[2]{0:T(128)S(1)}, bf16[64,1024]{1,0:T(8,128)(2,1)S(1)}, /*in...) while((s32[]{:T(128)}, f32[1,64,1024]{2,1,0:T(8,128)S(1)}, ...), condition=%wide.region_11.12_spmd.clone, body=%wide.region_9.11_spmd.clone.sunk | while | flops 229846016 | bytes 11594042 | solution.py:110
  375.8 0.6 dynamic_slice.68
  377.0 0.1 constant_dynamic-slice_fusion.5
  377.1 0.5 fusion.74
  377.6 2.1 multiply_reduce_fusion.3
  379.7 1.2 fusion.76
  380.9 0.3 fusion.75
  381.2 0.6 dynamic_slice.68
  382.5 0.1 constant_dynamic-slice_fusion.5
  382.6 0.5 fusion.74
  383.1 2.1 multiply_reduce_fusion.3
  385.2 1.2 fusion.76
  386.4 0.3 fusion.75
  386.7 0.0 copy-start
  386.7 0.7 copy-done
  387.4 0.0 all-reduce.5.cloned.1.call-update
  387.4 277.4 %psum.38 = f32[3,1024]{1,0:T(4,128)S(1)} all-reduce(f32[3,1024]{1,0:T(4,128)S(1)} %get-tuple-element.191), channel_id=1, replica_groups=mesh['head'=8,'ctx'=64] {'ctx'}, use_global_device_ids=true, to_apply=%region_13.14 | all-reduce | flops 3072 | bytes 24576 | tf_op jit(solution)/shard_map/psum | solution.py:113
  664.8 24.1 %psum.39 = f32[3,1024]{1,0:T(4,128)} all-reduce(f32[3,1024]{1,0:T(4,128)S(1)} %psum.38), channel_id=1, replica_groups=mesh['head'=8,'ctx'=64] {'head'}, use_global_device_ids=true, to_apply=%region_14.15 | all-reduce | flops 3072 | bytes 24576 | tf_op jit(solution)/shard_map/psum | solution.py:114
  688.9 0.0 all-reduce.5.cloned.1.call-done
  688.9 1.7 copy.58
  (21 shorter events, 0.2 us)
Async XLA Ops:
  7.2 65.7 %all-to-all-start = ((bf16[8,64,128]{2,1,0:T(8,128)(2,1)}), bf16[8,64,128]{2,1,0:T(8,128)(2,1)S(1)}, u32[]{:S(2)}, u32[]{:S(2)}) async-start(bf16[8,64,128]{2,1,0:T(8,128)(2,1)} %bitcast.131), calls=%async_computation | async-start | bytes 262144 | tf_op jit(solution)/shard_map/all_to_all | solution.py:13
  12.9 65.2 %copy-start.1 = (bf16[64,1024]{1,0:T(8,128)(2,1)S(1)}, bf16[64,1024]{1,0:T(8,128)(2,1)}, u32[]{:S(2)}) copy-start(bf16[64,1024]{1,0:T(8,128)(2,1)} %param.12) | copy-start | bytes 393220
  12.9 65.2 %copy-start.2 = (f32[3,1024]{1,0:T(4,128)S(1)}, f32[3,1024]{1,0:T(4,128)}, u32[]{:S(2)}) copy-start(f32[3,1024]{1,0:T(4,128)} %param.14) | copy-start | bytes 36868
  12.9 65.2 %copy-start.3 = (bf16[64,1024]{1,0:T(8,128)(2,1)S(1)}, bf16[64,1024]{1,0:T(8,128)(2,1)}, u32[]{:S(2)}) copy-start(bf16[64,1024]{1,0:T(8,128)(2,1)} %param.13) | copy-start | bytes 393220
  72.9 155.2 %all-to-all-start.1 = ((bf16[8,64,128]{2,1,0:T(8,128)(2,1)}), bf16[8,64,128]{2,1,0:T(8,128)(2,1)S(1)}, u32[]{:S(2)}, u32[]{:S(2)}) async-start(bf16[8,64,128]{2,1,0:T(8,128)(2,1)} %bitcast.6), calls=%async_computation.1 | async-start | bytes 262144 | tf_op jit(solution)/shard_map/all_to_all | solution.py:14
  77.9 296.2 %all-reduce.3.cloned.1.call-start = ((), (), s32[]{:S(2)}) async-start(), calls=%async_computation.2 | async-start | bytes 524288 | tf_op jit(solution)/shard_map/psum | solution.py:73
  227.3 461.6 %all-reduce.5.cloned.1.call-start = ((), (), s32[]{:S(2)}) async-start(), calls=%async_computation.3 | async-start | bytes 524288 | tf_op jit(solution)/shard_map/psum | solution.py:113
  386.7 0.7 copy-start
Sparse Core Ops, SparseCore 0:
  227.4 146.6 all-reduce.2
  387.5 148.3 all-reduce.4
